TPU v7x, 512 devices: a whole 4x4x16 slice. The times are simulated.
512 devices in a mesh: dp: 64 (over y, z), segment: 2 (over core), mp: 4 (over x).
Axes of the slice: x: 4, y: 4, z: 16, core: 2. Of those that a mesh axis runs over, the one named last changes fastest.
Arguments:
- hidden: bfloat16 [2, 512, 4096], P('segment', ('dp', 'mp')), may hold values from -6 to 6
- gain: float32 [4096], replicated, may hold values from 0.5 to 1.5
- head: bfloat16 [4096, 131072], P('segment', ('dp', 'mp')), may hold values from -0.09375 to 0.09375
- queries: bfloat16 [8, 131072], P(None, ('dp', 'mp')), may hold values from -48 to 48
- doc_spans: int32 [8], replicated, may hold values from 1 to 4, as said below
- labels: int32 [8], replicated, may hold values from 0 to 7
Outputs:
- grad_head: bfloat16 [4096, 131072], P('segment', ('dp', 'mp'))
- loss: float32 [], replicated
Inputs may be any that keep to these rules, and one draw needn't show every extreme that they name: `doc_spans`: the counts sum to 16; documents own consecutive spans in order; at least two documents have 4 spans.
All inputs are finite; a program needn't handle non-finite values.
Results may differ from a plain program's by a relative error of at most 0.008.
Values may be sent and summed in bfloat16 or wider, within the bound.
A program may use at most 64 MiB of HBM per device.

v0:
```python
import math
import jax
import jax.numpy as jnp
from jax import lax
from jax.sharding import PartitionSpec as P

V_DEV = 512
CH_MB = 8
NDOC = 8


def saturate(logits):
    return jnp.log1p(jax.nn.softplus(logits))


def slope(logits):
    return jax.nn.sigmoid(logits) / (1.0 + jax.nn.softplus(logits))


def row_norm(hidden, gain):
    values = hidden.astype(jnp.float32)
    mean_sq = jnp.mean(values * values, axis=-1, keepdims=True)
    return (values * lax.rsqrt(mean_sq + 1e-05) * gain).astype(jnp.bfloat16)


def owned_by(span_ids, bounds):
    inside = (span_ids[:, None] >= bounds[None, :-1]) & (span_ids[:, None] < bounds[None, 1:])
    return inside.astype(jnp.float32)


def shards(hidden, gain, head, queries, doc_spans, labels):
    width_dp = lax.axis_size("dp")
    width_mp = lax.axis_size("mp")
    segments = lax.axis_size("segment")
    vocab = V_DEV * width_dp * width_mp
    rows_here = hidden.shape[1]
    tok_mb = rows_here * width_dp * width_mp
    span = tok_mb // CH_MB
    micro_index = lax.axis_index("segment")
    normed = row_norm(hidden, gain)
    head_full = lax.all_gather(head, "segment", axis=0, tiled=True)
    bounds = jnp.concatenate([jnp.zeros((1,), jnp.int32), jnp.cumsum(doc_spans)])
    query_values = queries.astype(jnp.float32)
    scale = 1.0 / (math.sqrt(vocab) * span)

    def doc_table(count):
        span_ids = (micro_index * tok_mb + jnp.arange(count, dtype=jnp.int32)) // span
        return owned_by(span_ids, bounds)

    table = doc_table(tok_mb)
    rows = lax.all_gather(normed, ("dp", "mp"), axis=1, tiled=True)[0]
    block = jnp.dot(rows, head_full, preferred_element_type=jnp.float32)
    local_table = doc_table(rows.shape[0])
    pooled_now = jnp.dot(local_table.T, saturate(block), precision=lax.Precision.HIGHEST)
    pooled = pooled_now
    pooled = lax.psum(pooled, "segment")
    terms = jnp.dot(query_values, pooled.T, precision=lax.Precision.HIGHEST)
    scores = lax.psum(terms, ("dp", "mp")) * scale
    row_top = jnp.max(scores, axis=1, keepdims=True)
    log_total = row_top + jnp.log(jnp.sum(jnp.exp(scores - row_top), axis=1, keepdims=True))
    picks = (labels[:, None] == jnp.arange(NDOC, dtype=jnp.int32)[None, :]).astype(jnp.float32)
    loss = jnp.sum(log_total[:, 0] - jnp.sum(scores * picks, axis=1))
    score_grad = jnp.exp(scores - log_total) - picks
    pooled_grad = scale * jnp.dot(score_grad.T, query_values, precision=lax.Precision.HIGHEST)
    token_grad = jnp.dot(table, pooled_grad, precision=lax.Precision.HIGHEST)
    grad_scale = math.sqrt(vocab) * span / math.sqrt(segments * tok_mb)
    logit_grad = (token_grad * slope(block) * grad_scale).astype(jnp.bfloat16)
    rows = lax.all_gather(normed, ("dp", "mp"), axis=1, tiled=True)[0]
    summed = lax.dot_general(
        rows, logit_grad, (((0,), (0,)), ((), ())), preferred_element_type=jnp.float32
    )
    grad_head = lax.psum_scatter(
        summed.astype(jnp.bfloat16), "segment", scatter_dimension=0, tiled=True
    )
    return (grad_head, loss)


def solution(mesh):
    return jax.shard_map(
        shards,
        mesh=mesh,
        in_specs=(
            P("segment", ("dp", "mp"), None),
            P(),
            P("segment", ("dp", "mp")),
            P(None, ("dp", "mp")),
            P(),
            P(),
        ),
        out_specs=(P("segment", ("dp", "mp")), P()),
        check_vma=False,
    )
```

profile of v0, /device:TPU:1, one launch (start us, length us, event | category | flops | bytes accessed | tf_op | source)
XLA Modules:
  0.0 1000.5 jit_solution(7330918718881482748)
XLA Ops:
  7.2 0.0 copy-start
  7.2 0.0 all-gather.5.cloned.1.call-start
  7.2 0.7 all-gather.5.cloned.1.call-update
  7.9 0.0 all-gather.3.cloned.1.call-start
  8.0 0.9 fusion.16
  8.8 0.8 fusion.18
  9.7 0.6 copy.10
  10.3 0.0 all-gather.3.cloned.1.call-update
  10.3 0.0 reduce-scatter.2.cloned.1.call-start
  10.4 0.8 reduce-window.8
  11.2 0.1 pad_add_fusion
  11.3 0.0 copy-start.1
  11.3 29.7 %all-gather.5.cloned.1.call-done = bf16[4096,512]{1,0:T(8,128)(2,1)} async-done(((bf16[2048,512]{1,0:T(8,128)(2,1)}), bf16[4096,512]{1,0:T(8,128)(2,1)}) %all-gather.5.cloned.1.call-update) | async-done | bytes 4194320 | tf_op jit(solution)/shard_map/all_gather | solution.py:41
  41.0 216.8 %all-gather.3.cloned.1.call-done = bf16[1,512,4096]{2,0,1:T(2,128)(2,1)} async-done(((bf16[1,2,4096]{2,0,1:T(2,128)(2,1)}), bf16[1,512,4096]{2,0,1:T(2,128)(2,1)}) %all-gather.3.cloned.1.call-update) | async-done | bytes 4194320 | tf_op jit(solution)/shard_map/all_gather | solution.py:68
  257.8 9.3 fusion.1
  267.1 1.4 fusion.7
  268.5 11.3 %psum.14 = f32[8,512]{1,0:T(8,128)S(1)} all-reduce(f32[8,512]{1,0:T(8,128)S(1)} %fusion.7), channel_id=1, replica_groups=mesh['dp'=64,'segment'=2,'mp'=4] {'segment'}, use_global_device_ids=true, to_apply=%region_2.3 | all-reduce | flops 4096 | bytes 32768 | tf_op jit(solution)/shard_map/psum | solution.py:56
  279.7 0.0 copy-done
  279.7 0.1 convolution_bitcast_fusion
  279.9 577.1 %psum.15 = f32[8,8]{0,1:T(8,128)S(1)} all-reduce(f32[8,8]{0,1:T(8,128)S(1)} %convolution_bitcast_fusion), channel_id=1, replica_groups=mesh['dp'=64,'segment'=2,'mp'=4] {'dp','mp'}, use_global_device_ids=true, to_apply=%region_3.4 | all-reduce | flops 64 | bytes 512 | tf_op jit(solution)/shard_map/psum | solution.py:58
  857.0 0.0 copy-done.1
  857.0 0.6 subtract_reduce_fusion
  857.6 0.1 convolution_multiply_fusion.1
  857.7 1.4 fusion.6
  859.1 14.9 %convolution_convert_fusion = bf16[4096,512]{1,0:T(8,128)(2,1)} fusion(bf16[512,512]{1,0:T(8,128)(2,1)S(1)} %fusion.6, bf16[1,512,4096]{2,0,1:T(2,128)(2,1)} %all-gather.3.cloned.1.call-done), kind=kOutput, calls=%fused_computation | convolution fusion | flops 2149580800 | bytes 8912896 | tf_op jit(solution)/shard_map/dot_general | solution.py:69
  874.0 0.0 reduce-scatter.2.cloned.1.call-update
  874.0 119.9 %reduce-scatter.2.cloned.1.call-done = bf16[2048,512]{1,0:T(8,128)(2,1)} async-done(((bf16[4096,512]{1,0:T(8,128)(2,1)}), bf16[2048,512]{1,0:T(8,128)(2,1)}) %reduce-scatter.2.cloned.1.call-update) | async-done | bytes 2097168 | tf_op jit(solution)/shard_map/reduce_scatter | solution.py:72
  (4 shorter events, 0.1 us)
Async XLA Ops:
  7.2 272.6 %copy-start = (bf16[8,512]{1,0:T(8,128)(2,1)S(1)}, bf16[8,512]{1,0:T(8,128)(2,1)}, u32[]{:S(2)}) copy-start(bf16[8,512]{1,0:T(8,128)(2,1)} %param.9) | copy-start | bytes 24580
  7.2 33.8 %all-gather.5.cloned.1.call-start = ((), (), s32[]{:S(2)}) async-start(), calls=%async_computation.2 | async-start | bytes 6291456 | tf_op jit(solution)/shard_map/all_gather | solution.py:41
  7.9 249.9 %all-gather.3.cloned.1.call-start = ((), (), s32[]{:S(2)}) async-start(), calls=%async_computation.1 | async-start | bytes 8421376 | tf_op jit(solution)/shard_map/all_gather | solution.py:68
  10.3 983.7 %reduce-scatter.2.cloned.1.call-start = ((), (), s32[]{:S(2)}) async-start(), calls=%async_computation.3 | async-start | bytes 6291456 | tf_op jit(solution)/shard_map/reduce_scatter | solution.py:72
  11.3 845.7 %copy-start.1 = (s32[8]{0:T(128)S(1)}, s32[8]{0:T(128)}, u32[]{:S(2)}) copy-start(s32[8]{0:T(128)} %param.11) | copy-start | bytes 100
Sparse Core Ops, SparseCore 0:
  10.1 30.8 all-gather.4
  46.2 211.6 all-gather.2
  874.2 119.7 reduce-scatter.1
where the time goes:
time: 1000 us
  blocking collectives  588 us (59%)
  waiting for transfers between devices  367 us (37%)
  matrix products  27.1 us (3%)
  between operations  13.8 us (1%)
    psum x1, blocking collectives, shards(): scores = lax.psum(terms, ('dp', 'mp')) * scale  577 us
    all_gather x1, waiting for transfers between devices, shards(): rows = lax.all_gather(normed, ('dp', 'mp'), axis=1, tiled=True)[0]  217 us
    reduce_scatter x1, waiting for transfers between devices, shards(): lax.psum_scatter(summed.astype(jnp.bfloat16), 'segment', scatter_dimensio...  120 us
    all_gather x1, waiting for transfers between devices, shards(): head_full = lax.all_gather(head, 'segment', axis=0, tiled=True)  29.7 us
  transfers between devices with their start and end apart: 3, of which 3 were waited for; matrix products, arithmetic and copies ran while one was open for 0% of the time, Pallas kernels for 0%

commit v1 on v0

--- a/solution.py
+++ b/solution.py
@@ -7,6 +7,7 @@
 V_DEV = 512
 CH_MB = 8
 NDOC = 8
+test_run_for = lambda x0: lax.psum(lax.psum(x0, axis_name="dp"), axis_name="mp")
 
 
 def saturate(logits):
@@ -55,7 +56,7 @@
     pooled = pooled_now
     pooled = lax.psum(pooled, "segment")
     terms = jnp.dot(query_values, pooled.T, precision=lax.Precision.HIGHEST)
-    scores = lax.psum(terms, ("dp", "mp")) * scale
+    scores = test_run_for(terms) * scale
     row_top = jnp.max(scores, axis=1, keepdims=True)
     log_total = row_top + jnp.log(jnp.sum(jnp.exp(scores - row_top), axis=1, keepdims=True))
     picks = (labels[:, None] == jnp.arange(NDOC, dtype=jnp.int32)[None, :]).astype(jnp.float32)

time: 1000 us -> 465 us (0.47)
  blocking collectives: 588 us -> 133 us
  waiting for transfers between devices: 367 us -> 287 us
    psum x1 -> x2, blocking collectives: 577 us -> 121 us  [the longest x1 115 us: lax.psum(x0, axis_name='dp')]
    reduce_scatter x1, waiting for transfers between devices: 120 us -> 40 us  [shards(): lax.psum_scatter(summed.astype(jnp.bfloat16), 'segment', scatter_dimensio...]
  transfers between devices with their start and end apart: 3 -> 3, of which waited for: 3 -> 3; matrix products, arithmetic and copies ran while one was open for 0% -> 1% of each run, Pallas kernels for 0% -> 0%
where the time goes in v1:
time: 465 us
  waiting for transfers between devices  287 us (62%)
  blocking collectives  133 us (29%)
  matrix products  27.1 us (6%)
  between operations  13.8 us (3%)
    all_gather x1, waiting for transfers between devices, shards(): rows = lax.all_gather(normed, ('dp', 'mp'), axis=1, tiled=True)[0]  217 us
    psum x1, blocking collectives, lax.psum(x0, axis_name='dp')  115 us
    reduce_scatter x1, waiting for transfers between devices, shards(): lax.psum_scatter(summed.astype(jnp.bfloat16), 'segment', scatter_dimensio...  40 us
    all_gather x1, waiting for transfers between devices, shards(): head_full = lax.all_gather(head, 'segment', axis=0, tiled=True)  29.7 us
    dot_general x1, matrix products, shards(): lax.dot_general(rows, logit_grad, (((0,), (0,)), ((), ())), preferred_ele...  14.9 us
    psum x1, blocking collectives, shards(): pooled = lax.psum(pooled, 'segment')  11.3 us
  transfers between devices with their start and end apart: 3, of which 3 were waited for; matrix products, arithmetic and copies ran while one was open for 1% of the time, Pallas kernels for 0%

profile of v1, /device:TPU:1, one launch (start us, length us, event | category | flops | bytes accessed | tf_op | source)
XLA Modules:
  0.0 464.9 jit_solution(7281263343579018955)
XLA Ops:
  7.2 0.0 copy-start
  7.2 0.0 all-gather.5.cloned.1.call-start
  7.2 0.7 all-gather.5.cloned.1.call-update
  7.9 0.0 all-gather.3.cloned.1.call-start
  8.0 0.9 fusion.16
  8.8 0.8 fusion.18
  9.7 0.6 copy.10
  10.3 0.0 all-gather.3.cloned.1.call-update
  10.3 0.0 reduce-scatter.2.cloned.1.call-start
  10.4 0.8 reduce-window.8
  11.2 0.1 pad_add_fusion
  11.3 0.0 copy-start.1
  11.3 29.7 %all-gather.5.cloned.1.call-done = bf16[4096,512]{1,0:T(8,128)(2,1)} async-done(((bf16[2048,512]{1,0:T(8,128)(2,1)}), bf16[4096,512]{1,0:T(8,128)(2,1)}) %all-gather.5.cloned.1.call-update) | async-done | bytes 4194320 | tf_op jit(solution)/shard_map/all_gather | solution.py:42
  41.0 216.8 %all-gather.3.cloned.1.call-done = bf16[1,512,4096]{2,0,1:T(2,128)(2,1)} async-done(((bf16[1,2,4096]{2,0,1:T(2,128)(2,1)}), bf16[1,512,4096]{2,0,1:T(2,128)(2,1)}) %all-gather.3.cloned.1.call-update) | async-done | bytes 4194320 | tf_op jit(solution)/shard_map/all_gather | solution.py:69
  257.8 9.3 %fusion.1 = f32[512,512]{1,0:T(8,128)S(1)} fusion(bf16[4096,512]{1,0:T(8,128)(2,1)} %all-gather.5.cloned.1.call-done, bf16[1,512,4096]{2,0,1:T(2,128)(2,1)} %all-gather.3.cloned.1.call-done), kind=kOutput, calls=%fused_computation.2 | convolution fusion | flops 2147483648 | bytes 9437184 | tf_op jit(solution)/shard_map/dot_general | solution.py:53
  267.1 1.4 fusion.7
  268.5 11.3 %psum.21 = f32[8,512]{1,0:T(8,128)S(1)} all-reduce(f32[8,512]{1,0:T(8,128)S(1)} %fusion.7), channel_id=1, replica_groups=mesh['dp'=64,'segment'=2,'mp'=4] {'segment'}, use_global_device_ids=true, to_apply=%region_2.3 | all-reduce | flops 4096 | bytes 32768 | tf_op jit(solution)/shard_map/psum | solution.py:57
  279.7 0.0 copy-done
  279.7 0.1 convolution_bitcast_fusion
  279.9 115.1 %psum.22 = f32[8,8]{0,1:T(8,128)S(1)} all-reduce(f32[8,8]{0,1:T(8,128)S(1)} %convolution_bitcast_fusion), channel_id=1, replica_groups=mesh['dp'=64,'segment'=2,'mp'=4] {'dp'}, use_global_device_ids=true, to_apply=%region_3.4 | all-reduce | flops 64 | bytes 512 | tf_op jit(solution)/shard_map/psum | solution.py:10
  395.0 6.3 %psum.23 = f32[8,8]{0,1:T(8,128)S(1)} all-reduce(f32[8,8]{0,1:T(8,128)S(1)} %psum.22), channel_id=1, replica_groups=mesh['dp'=64,'segment'=2,'mp'=4] {'mp'}, use_global_device_ids=true, to_apply=%region_4.5 | all-reduce | flops 64 | bytes 512 | tf_op jit(solution)/shard_map/psum | solution.py:10
  401.4 0.0 copy-done.1
  401.4 0.6 subtract_reduce_fusion
  402.0 0.1 convolution_multiply_fusion.1
  402.1 1.4 fusion.6
  403.5 14.9 %convolution_convert_fusion = bf16[4096,512]{1,0:T(8,128)(2,1)} fusion(bf16[512,512]{1,0:T(8,128)(2,1)S(1)} %fusion.6, bf16[1,512,4096]{2,0,1:T(2,128)(2,1)} %all-gather.3.cloned.1.call-done), kind=kOutput, calls=%fused_computation | convolution fusion | flops 2149580800 | bytes 8912896 | tf_op jit(solution)/shard_map/dot_general | solution.py:70
  418.4 0.0 reduce-scatter.2.cloned.1.call-update
  418.4 40.0 %reduce-scatter.2.cloned.1.call-done = bf16[2048,512]{1,0:T(8,128)(2,1)} async-done(((bf16[4096,512]{1,0:T(8,128)(2,1)}), bf16[2048,512]{1,0:T(8,128)(2,1)}) %reduce-scatter.2.cloned.1.call-update) | async-done | bytes 2097168 | tf_op jit(solution)/shard_map/reduce_scatter | solution.py:73
  (4 shorter events, 0.1 us)
Async XLA Ops:
  7.2 272.6 %copy-start = (bf16[8,512]{1,0:T(8,128)(2,1)S(1)}, bf16[8,512]{1,0:T(8,128)(2,1)}, u32[]{:S(2)}) copy-start(bf16[8,512]{1,0:T(8,128)(2,1)} %param.9) | copy-start | bytes 24580
  7.2 33.8 %all-gather.5.cloned.1.call-start = ((), (), s32[]{:S(2)}) async-start(), calls=%async_computation.2 | async-start | bytes 6291456 | tf_op jit(solution)/shard_map/all_gather | solution.py:42
  7.9 249.9 %all-gather.3.cloned.1.call-start = ((), (), s32[]{:S(2)}) async-start(), calls=%async_computation.1 | async-start | bytes 8421376 | tf_op jit(solution)/shard_map/all_gather | solution.py:69
  10.3 448.1 %reduce-scatter.2.cloned.1.call-start = ((), (), s32[]{:S(2)}) async-start(), calls=%async_computation.3 | async-start | bytes 6291456 | tf_op jit(solution)/shard_map/reduce_scatter | solution.py:73
  11.3 390.0 %copy-start.1 = (s32[8]{0:T(128)S(1)}, s32[8]{0:T(128)}, u32[]{:S(2)}) copy-start(s32[8]{0:T(128)} %param.11) | copy-start | bytes 100
Sparse Core Ops, SparseCore 0:
  10.1 30.8 all-gather.4
  46.2 211.6 all-gather.2
  418.5 39.8 reduce-scatter.1
